TPU v7x, 512 devices: a whole 4x8x8 slice. The times are simulated.
512 devices in a mesh: outer: 16 (over y_lo, z), inner: 32 (over x, y_hi, core).
Axes of the slice: x: 4, y: 8 (y_hi: 4, y_lo: 2; y = y_hi * 2 + y_lo), z: 8, core: 2. Of those that a mesh axis runs over, the one named last changes fastest.
Arguments:
- queries: bfloat16 [65536, 8192], P(('outer', 'inner')), may hold values from -8 to 8
- keys: bfloat16 [65536, 512], P(('outer', 'inner')), may hold values from -8 to 8
- values: bfloat16 [65536, 512], P(('outer', 'inner')), may hold values from -6 to 6
- doc_ids: int32 [65536], P(('outer', 'inner')), may hold values from 0 to 3, never falling along the last dimension, each value on 1 to 32768 neighbouring positions
Outputs:
- attended: bfloat16 [65536, 8192], P(('outer', 'inner'))
- log_norm: float32 [64, 65536], P(None, ('outer', 'inner'))
Inputs may be any that keep to these rules, and one draw needn't show every extreme that they name: `doc_ids`: document numbers never fall along the sequence; each document is 1 to 32768 tokens.
All inputs are finite; a program needn't handle non-finite values.
Results may differ from a plain program's by a relative error of at most 0.006.
Values may be sent and summed in bfloat16 or wider, within the bound.
A program may use at most 128 MiB of HBM per device.

v0:
```python
import jax
import jax.numpy as jnp
from jax import lax
from jax.sharding import PartitionSpec as P

HEAD_WIDTH = 128


floor_score = -1e30


def from_behind(block, axis, distance):
    devices = range(lax.axis_size(axis))
    route = [(i - distance, i) for i in devices if i - distance in devices]
    return lax.ppermute(block, axis, route)


def block_terms(query_split, key_block, value_block, visible):
    rows = key_block.shape[0]
    key_heads = key_block.shape[1] // HEAD_WIDTH
    key_split = key_block.reshape(rows, key_heads, HEAD_WIDTH)
    value_split = value_block.reshape(rows, key_heads, HEAD_WIDTH)
    scores = jnp.einsum(
        "tkgd,jkd->kgtj", query_split, key_split, preferred_element_type=jnp.float32
    ) * HEAD_WIDTH ** (-0.5)
    masked = jnp.where(visible, scores, floor_score)
    peak = jnp.max(masked, axis=-1)
    weights = jnp.where(visible, jnp.exp(scores - peak[..., None]), 0.0).astype(jnp.bfloat16)
    total = jnp.sum(weights.astype(jnp.float32), axis=-1)
    weighted = jnp.einsum(
        "kgtj,jkd->tkgd", weights, value_split, preferred_element_type=jnp.float32
    )
    return (peak, total, weighted)


def combine(state, fresh):
    peak_old, total_old, sum_old = state
    peak_new, total_new, sum_new = fresh
    peak = jnp.maximum(peak_old, peak_new)
    scale_old = jnp.exp(peak_old - peak)
    scale_new = jnp.exp(peak_new - peak)
    total = scale_old * total_old + scale_new * total_new
    weighted = (
        jnp.transpose(scale_old, (2, 0, 1))[..., None] * sum_old
        + jnp.transpose(scale_new, (2, 0, 1))[..., None] * sum_new
    )
    return (peak, total, weighted)


def on_device(queries, keys, values, doc_ids):
    rows = queries.shape[0]
    key_heads = keys.shape[1] // HEAD_WIDTH
    group = queries.shape[1] // keys.shape[1]
    inner_count = lax.axis_size("inner")
    place = lax.axis_index("outer") * inner_count + lax.axis_index("inner")
    query_split = queries.reshape(rows, key_heads, group, HEAD_WIDTH)
    local = jnp.arange(rows, dtype=jnp.int32)
    causal = local[:, None] >= local[None, :]
    near_keys, near_values, near_docs = from_behind((keys, values, doc_ids), ("outer", "inner"), 1)
    far_keys, far_values, far_docs = from_behind((keys, values, doc_ids), "outer", 1)
    second_keys, second_values, second_docs = from_behind(
        (keys, values, doc_ids), ("outer", "inner"), 2
    )
    distant_keys, distant_values, distant_docs = from_behind((keys, values, doc_ids), "outer", 2)
    own_visible = causal & (doc_ids[:, None] == doc_ids[None, :])
    state = block_terms(query_split, keys, values, own_visible)
    remote = [
        (near_keys, near_values, near_docs, 1),
        (second_keys, second_values, second_docs, 2),
        (far_keys, far_values, far_docs, inner_count),
        (distant_keys, distant_values, distant_docs, 2 * inner_count),
    ]
    for key_block, value_block, key_docs, offset in remote:
        visible = (doc_ids[:, None] == key_docs[None, :]) & (place >= offset)
        state = combine(state, block_terms(query_split, key_block, value_block, visible))
    peak, total, weighted = state
    attended = (
        (weighted / jnp.transpose(total, (2, 0, 1))[..., None])
        .reshape(rows, -1)
        .astype(jnp.bfloat16)
    )
    log_norm = (peak + jnp.log(total)).reshape(-1, rows)
    return (attended, log_norm)


def solution(mesh):
    in_specs = (
        P(("outer", "inner"), None),
        P(("outer", "inner"), None),
        P(("outer", "inner"), None),
        P(("outer", "inner")),
    )
    out_specs = (P(("outer", "inner"), None), P(None, ("outer", "inner")))
    return jax.shard_map(
        on_device, mesh=mesh, in_specs=in_specs, out_specs=out_specs, check_vma=False
    )
```

profile of v0, /device:TPU:64, one launch (start us, length us, event | category | flops | bytes accessed | tf_op | source)
XLA Modules:
  0.0 109.2 jit_solution(6491283243450160326)
XLA Ops:
  0.6 0.0 copy-start.4
  0.7 2.1 %collective-permute-start = (s32[128]{0:T(128)}, s32[128]{0:T(128)S(1)}, u32[]{:S(2)}, u32[]{:S(2)}) collective-permute-start(s32[128]{0:T(128)} %param.7), channel_id=1, source_target_pairs={{0,1},{1,2},{2,3},{3,4},{4,5},{5,6},{6,7},{7,8},{8,9},{9,10},{10,1... | collective-permute-start | bytes 1544 | tf_op jit(solution)/shard_map/ppermute | solution.py:15
  2.7 4.5 %collective-permute-start.2 = (s32[128]{0:T(128)}, s32[128]{0:T(128)S(1)}, u32[]{:S(2)}, u32[]{:S(2)}) collective-permute-start(s32[128]{0:T(128)} %param.7), channel_id=1, source_target_pairs={{0,2},{1,3},{2,4},{3,5},{4,6},{5,7},{6,8},{7,9},{8,10},{9,11},{10,... | collective-permute-start | bytes 1544 | tf_op jit(solution)/shard_map/ppermute | solution.py:15
  7.2 6.1 %collective-permute-start.6 = (s32[128]{0:T(128)}, s32[128]{0:T(128)S(1)}, u32[]{:S(2)}, u32[]{:S(2)}) collective-permute-start(s32[128]{0:T(128)} %param.7), channel_id=1, source_target_pairs={{0,64},{32,96},{64,128},{96,160},{128,192},{160,224},{192,256},{22... | collective-permute-start | bytes 1544 | tf_op jit(solution)/shard_map/ppermute | solution.py:15
  13.3 5.5 %collective-permute-start.4 = (s32[128]{0:T(128)}, s32[128]{0:T(128)S(1)}, u32[]{:S(2)}, u32[]{:S(2)}) collective-permute-start(s32[128]{0:T(128)} %param.7), channel_id=1, source_target_pairs={{0,32},{32,64},{64,96},{96,128},{128,160},{160,192},{192,224},{224... | collective-permute-start | bytes 1544 | tf_op jit(solution)/shard_map/ppermute | solution.py:15
  18.8 1.0 copy.25
  19.8 4.3 %collective-permute-start.7 = (bf16[128,512]{0,1:T(8,128)(2,1)S(1)}, bf16[128,512]{0,1:T(8,128)(2,1)S(1)}, u32[]{:S(2)}, u32[]{:S(2)}) collective-permute-start(bf16[128,512]{0,1:T(8,128)(2,1)S(1)} %copy.25), channel_id=1, source_target_pairs={{0,64},{32,96},{64,128},{96,160},{128,192},{160,224},{192,256},{22... | collective-permute-start | bytes 393224 | tf_op jit(solution)/shard_map/ppermute | solution.py:15
  24.1 0.9 reshape.70
  25.1 1.0 copy.73
  26.1 2.2 %copy.74 = bf16[16,8,64,128]{3,2,1,0:T(8,128)(2,1)S(1)} copy(bf16[16,8,64,128]{3,1,2,0:T(8,128)(2,1)} %bitcast.360) | data formatting | bytes 4194304
  28.3 0.0 collective-permute-done
  28.3 3.4 %collective-permute-start.5 = (bf16[128,512]{0,1:T(8,128)(2,1)S(1)}, bf16[128,512]{0,1:T(8,128)(2,1)S(1)}, u32[]{:S(2)}, u32[]{:S(2)}) collective-permute-start(bf16[128,512]{0,1:T(8,128)(2,1)S(1)} %copy.25), channel_id=1, source_target_pairs={{0,32},{32,64},{64,96},{96,128},{128,160},{160,192},{192,224},{224... | collective-permute-start | bytes 393224 | tf_op jit(solution)/shard_map/ppermute | solution.py:15
  31.7 0.0 collective-permute-done.2
  31.7 5.7 %collective-permute-start.3 = (bf16[128,512]{0,1:T(8,128)(2,1)S(1)}, bf16[128,512]{0,1:T(8,128)(2,1)S(1)}, u32[]{:S(2)}, u32[]{:S(2)}) collective-permute-start(bf16[128,512]{0,1:T(8,128)(2,1)S(1)} %copy.25), channel_id=1, source_target_pairs={{0,2},{1,3},{2,4},{3,5},{4,6},{5,7},{6,8},{7,9},{8,10},{9,11},{10,... | collective-permute-start | bytes 393224 | tf_op jit(solution)/shard_map/ppermute | solution.py:15
  37.5 0.0 collective-permute-done.6
  37.5 1.9 %collective-permute-start.1 = (bf16[128,512]{0,1:T(8,128)(2,1)S(1)}, bf16[128,512]{0,1:T(8,128)(2,1)S(1)}, u32[]{:S(2)}, u32[]{:S(2)}) collective-permute-start(bf16[128,512]{0,1:T(8,128)(2,1)S(1)} %copy.25), channel_id=1, source_target_pairs={{0,1},{1,2},{2,3},{3,4},{4,5},{5,6},{6,7},{7,8},{8,9},{9,10},{10,1... | collective-permute-start | bytes 393224 | tf_op jit(solution)/shard_map/ppermute | solution.py:15
  39.4 0.0 collective-permute-done.4
  39.4 2.7 %collective-permute-start.9 = (bf16[128,512]{1,0:T(8,128)(2,1)S(1)}, bf16[128,512]{1,0:T(8,128)(2,1)S(1)}, u32[]{:S(2)}, u32[]{:S(2)}) collective-permute-start(bf16[128,512]{1,0:T(8,128)(2,1)S(1)} %copy-done.4), channel_id=1, source_target_pairs={{0,2},{1,3},{2,4},{3,5},{4,6},{5,7},{6,8},{7,9},{8,10},{9,11},{10,... | collective-permute-start | bytes 393224 | tf_op jit(solution)/shard_map/ppermute | solution.py:15
  42.1 0.2 compare_and_fusion
  42.3 2.1 %fusion.25 = (f32[4,16,128]{2,1,0:T(8,128)S(1)}, f32[4,128,128,16]{2,1,3,0:T(8,128)S(1)}) fusion(pred[128,128]{0,1:T(8,128)(4,1)S(1)} %get-tuple-element.19, bf16[128,4,16,128]{3,2,1,0:T(8,128)(2,1)S(1)} %bitcast.355, bf16[128,4,128,1]{2,1,0,3:T(4,128)(2,1)S(1)} %bitcast.366), kind=kOutput, calls=%fused_computation.40 | convolution fusion | flops 271572992 | bytes 6471680 | tf_op jit(solution)/shard_map/tkgd,jkd->kgtj/dot_general | solution.py:23
  44.4 2.8 %fusion.75 = f32[4,16,128,128]{2,3,1,0:T(8,128)} fusion(bf16[128,4,128,1]{0,2,3,1:T(8,128)(2,1)S(1)} %bitcast.362, f32[4,128,128,16]{2,1,3,0:T(8,128)S(1)} %get-tuple-element.27, f32[4,16,128]{2,1,0:T(8,128)S(1)} %get-tuple-element.26, pred[128,128]{0,1:T(8,128)(4,1)S(1)} %get-tuple-element.19), kind=kOutput, calls=%fused_computation.129 | convolution fusion | flops 272629760 | bytes 8568832 | tf_op jit(solution)/shard_map/kgtj,jkd->tkgd/dot_general | solution.py:30
  47.2 1.2 %convert_reduce_fusion.4 = f32[4,16,128]{2,1,0:T(8,128)S(1)} fusion(f32[4,16,128]{2,1,0:T(8,128)S(1)} %get-tuple-element.26, f32[4,128,128,16]{2,1,3,0:T(8,128)S(1)} %get-tuple-element.27, pred[128,128]{0,1:T(8,128)(4,1)S(1)} %get-tuple-element.19), kind=kLoop, calls=%fused_computation.48 | loop fusion | flops 6283264 | bytes 4276224 | tf_op jit(solution)/shard_map/reduce_sum | solution.py:29
  48.3 7.7 %collective-permute-done.1 = bf16[128,512]{0,1:T(8,128)(2,1)S(1)} collective-permute-done((bf16[128,512]{0,1:T(8,128)(2,1)S(1)}, bf16[128,512]{0,1:T(8,128)(2,1)S(1)}, u32[]{:S(2)}, u32[]{:S(2)}) %collective-permute-start.1) | collective-permute-done | bytes 131104 | tf_op jit(solution)/shard_map/ppermute | solution.py:15
  56.0 1.9 %collective-permute-start.8 = (bf16[128,512]{1,0:T(8,128)(2,1)S(1)}, bf16[128,512]{1,0:T(8,128)(2,1)S(1)}, u32[]{:S(2)}, u32[]{:S(2)}) collective-permute-start(bf16[128,512]{1,0:T(8,128)(2,1)S(1)} %copy-done.4), channel_id=1, source_target_pairs={{0,1},{1,2},{2,3},{3,4},{4,5},{5,6},{6,7},{7,8},{8,9},{9,10},{10,1... | collective-permute-start | bytes 393224 | tf_op jit(solution)/shard_map/ppermute | solution.py:15
  58.0 2.0 %fusion.21 = (f32[4,16,128]{2,1,0:T(8,128)S(1)}, f32[4,128,128,16]{2,1,3,0:T(8,128)S(1)}) fusion(pred[128,128]{0,1:T(8,128)(4,1)S(1)} %get-tuple-element.18, bf16[128,4,128,1]{0,2,3,1:T(8,128)(2,1)S(1)} %bitcast.370, bf16[128,4,16,128]{3,2,1,0:T(8,128)(2,1)S(1)} %bitcast.356), kind=kOutput, calls=%fused_computation.34 | convolution fusion | flops 271572992 | bytes 6471680 | tf_op jit(solution)/shard_map/tkgd,jkd->kgtj/dot_general | solution.py:23
  60.0 0.0 collective-permute-done.3
  60.0 1.3 %collective-permute-start.11 = (bf16[128,512]{1,0:T(8,128)(2,1)S(1)}, bf16[128,512]{1,0:T(8,128)(2,1)S(1)}, u32[]{:S(2)}, u32[]{:S(2)}) collective-permute-start(bf16[128,512]{1,0:T(8,128)(2,1)S(1)} %copy-done.4), channel_id=1, source_target_pairs={{0,64},{32,96},{64,128},{96,160},{128,192},{160,224},{192,256},{22... | collective-permute-start | bytes 393224 | tf_op jit(solution)/shard_map/ppermute | solution.py:15
  61.3 2.0 %fusion.17 = (f32[4,16,128]{2,1,0:T(8,128)S(1)}, f32[4,128,128,16]{2,1,3,0:T(8,128)S(1)}) fusion(pred[128,128]{0,1:T(8,128)(4,1)S(1)} %get-tuple-element.16, bf16[128,4,128,1]{0,2,3,1:T(8,128)(2,1)S(1)} %bitcast.369, bf16[128,4,16,128]{3,2,1,0:T(8,128)(2,1)S(1)} %bitcast.357), kind=kOutput, calls=%fused_computation.28 | convolution fusion | flops 271572992 | bytes 6471680 | tf_op jit(solution)/shard_map/tkgd,jkd->kgtj/dot_general | solution.py:23
  63.4 2.5 %convert_reduce_fusion.2 = (f32[4,16,128]{2,1,0:T(8,128)S(1)}, f32[4,16,128]{2,1,0:T(8,128)S(1)}) fusion(f32[4,16,128]{2,1,0:T(8,128)S(1)} %get-tuple-element.22, f32[4,128,128,16]{2,1,3,0:T(8,128)S(1)} %get-tuple-element.23, pred[128,128]{0,1:T(8,128)(4,1)S(1)} %get-tuple-element.16, f32[4,16,128]{2,1,0:T(8,128)S(1)} %get-tuple-element.24, ...), kind=kLoop, calls=%fused_computation.46 | loop fusion | flops 12566528 | bytes 8552448 | tf_op jit(solution)/shard_map/reduce_sum | solution.py:29
  65.9 1.6 %collective-permute-done.8 = bf16[128,512]{1,0:T(8,128)(2,1)S(1)} collective-permute-done((bf16[128,512]{1,0:T(8,128)(2,1)S(1)}, bf16[128,512]{1,0:T(8,128)(2,1)S(1)}, u32[]{:S(2)}, u32[]{:S(2)}) %collective-permute-start.8) | collective-permute-done | bytes 131104 | tf_op jit(solution)/shard_map/ppermute | solution.py:15
  67.5 2.1 %collective-permute-start.10 = (bf16[128,512]{1,0:T(8,128)(2,1)S(1)}, bf16[128,512]{1,0:T(8,128)(2,1)S(1)}, u32[]{:S(2)}, u32[]{:S(2)}) collective-permute-start(bf16[128,512]{1,0:T(8,128)(2,1)S(1)} %copy-done.4), channel_id=1, source_target_pairs={{0,32},{32,64},{64,96},{96,128},{128,160},{160,192},{192,224},{224... | collective-permute-start | bytes 393224 | tf_op jit(solution)/shard_map/ppermute | solution.py:15
  69.6 0.1 copy.39
  69.8 5.0 %fusion.77 = f32[4,16,128,128]{2,3,1,0:T(8,128)} fusion(bf16[128,4,128,1]{0,2,3,1:T(8,128)(2,1)S(1)} %bitcast.363, f32[4,128,128,16]{2,1,3,0:T(8,128)} %copy-done, f32[4,16,128]{2,1,0:T(8,128)S(1)} %get-tuple-element.24, pred[128,128]{0,1:T(8,128)(4,1)S(1)} %get-tuple-element.18), kind=kOutput, calls=%fused_computation.130 | convolution fusion | flops 272629760 | bytes 8568832 | tf_op jit(solution)/shard_map/kgtj,jkd->tkgd/dot_general | solution.py:30
  74.8 0.1 copy.41
  74.9 5.0 %fusion.79 = f32[4,16,128,128]{2,3,1,0:T(8,128)} fusion(bf16[128,4,128,1]{0,2,3,1:T(8,128)(2,1)S(1)} %bitcast.364, f32[4,128,128,16]{2,1,3,0:T(8,128)} %copy-done.1, f32[4,16,128]{2,1,0:T(8,128)S(1)} %get-tuple-element.22, pred[128,128]{0,1:T(8,128)(4,1)S(1)} %get-tuple-element.16), kind=kOutput, calls=%fused_computation.131 | convolution fusion | flops 272629760 | bytes 8568832 | tf_op jit(solution)/shard_map/kgtj,jkd->tkgd/dot_general | solution.py:30
  79.9 0.0 collective-permute-done.5
  79.9 4.0 %fusion.13 = (f32[4,16,128]{2,1,0:T(8,128)S(1)}, f32[4,128,128,16]{2,1,3,0:T(8,128)}) fusion(pred[128,128]{0,1:T(8,128)(4,1)S(1)} %get-tuple-element.17, bf16[128,4,128,1]{0,2,3,1:T(8,128)(2,1)S(1)} %bitcast.368, bf16[128,4,16,128]{3,2,1,0:T(8,128)(2,1)S(1)} %bitcast.358), kind=kOutput, calls=%fused_computation.22 | convolution fusion | flops 271572992 | bytes 6471680 | tf_op jit(solution)/shard_map/tkgd,jkd->kgtj/dot_general | solution.py:23
  83.8 0.0 collective-permute-done.7
  83.8 3.9 %fusion.9 = (f32[4,16,128]{2,1,0:T(8,128)S(1)}, f32[4,128,128,16]{2,1,3,0:T(8,128)}) fusion(pred[128,128]{0,1:T(8,128)(4,1)S(1)} %get-tuple-element.15, bf16[128,4,128,1]{0,2,3,1:T(8,128)(2,1)S(1)} %bitcast.367, bf16[128,4,16,128]{3,2,1,0:T(8,128)(2,1)S(1)} %bitcast.359), kind=kOutput, calls=%fused_computation.16 | convolution fusion | flops 271572992 | bytes 6471680 | tf_op jit(solution)/shard_map/tkgd,jkd->kgtj/dot_general | solution.py:23
  87.7 0.1 copy.43
  87.9 5.2 %fusion.81 = f32[4,16,128,128]{2,3,1,0:T(8,128)} fusion(bf16[128,4,128,1]{0,2,3,1:T(8,128)(2,1)S(1)} %bitcast.365, f32[4,128,128,16]{2,1,3,0:T(8,128)} %get-tuple-element.21, f32[4,16,128]{2,1,0:T(8,128)S(1)} %get-tuple-element.20, pred[128,128]{0,1:T(8,128)(4,1)S(1)} %get-tuple-element.17), kind=kOutput, calls=%fused_computation.132 | convolution fusion | flops 272629760 | bytes 8568832 | tf_op jit(solution)/shard_map/kgtj,jkd->tkgd/dot_general | solution.py:30
  93.1 0.8 copy-done.3
  93.9 2.5 %convert_reduce_fusion = (f32[4,16,128]{2,1,0:T(8,128)S(1)}, f32[4,16,128]{2,1,0:T(8,128)S(1)}) fusion(f32[4,16,128]{2,1,0:T(8,128)S(1)} %get-tuple-element.28, f32[4,128,128,16]{2,1,3,0:T(8,128)S(1)} %copy-done.3, pred[128,128]{0,1:T(8,128)(4,1)S(1)} %get-tuple-element.15, f32[4,16,128]{2,1,0:T(8,128)S(1)} %get-tuple-element.20, ...), kind=kLoop, calls=%fused_computation.44 | loop fusion | flops 12566528 | bytes 8552448 | tf_op jit(solution)/shard_map/reduce_sum | solution.py:29
  96.4 0.1 fusion.64
  96.4 0.7 fusion.45
  97.1 0.1 copy.45
  97.2 9.0 %fusion.2 = bf16[128,4,16,128]{0,3,2,1:T(8,128)(2,1)S(1)} fusion(f32[4,16,128,128]{2,3,1,0:T(8,128)} %fusion.81, f32[4,16,128,128]{2,3,1,0:T(8,128)} %fusion.79, f32[4,16,128,128]{2,3,1,0:T(8,128)} %fusion.77, f32[4,16,128,128]{2,3,1,0:T(8,128)} %fusion.75, bf16[128,4,128,1]{0,2,3,1:T(8,128)(2,1)S(1)} %bitcast.371, f32[128,4,16]{0,2,1:T(8,128)S(1)} %get-tuple-element.6, ...), kind=kOutput, calls=%fused_computation.3 | convolution fusion | flops 287309824 | bytes 23543808 | tf_op jit(solution)/shard_map/kgtj,jkd->tkgd/dot_general | solution.py:30
  106.3 2.9 %copy.47 = bf16[128,8192]{1,0:T(8,128)(2,1)} copy(bf16[128,8192]{0,1:T(8,128)(2,1)S(1)} %bitcast.361) | data formatting | bytes 4194304
  (13 shorter events, 0.0 us)
Async XLA Ops:
  0.6 41.5 %copy-start.5 = (s32[128]{0:T(128)S(1)}, s32[128]{0:T(128)}, u32[]{:S(2)}) copy-start(s32[128]{0:T(128)} %param.7) | copy-start | bytes 1540
  0.6 38.8 %copy-start.4 = (bf16[128,512]{1,0:T(8,128)(2,1)S(1)}, bf16[128,512]{1,0:T(8,128)(2,1)}, u32[]{:S(2)}) copy-start(bf16[128,512]{1,0:T(8,128)(2,1)} %param.6) | copy-start | bytes 393220
  0.7 27.7 %collective-permute-start = (s32[128]{0:T(128)}, s32[128]{0:T(128)S(1)}, u32[]{:S(2)}, u32[]{:S(2)}) collective-permute-start(s32[128]{0:T(128)} %param.7), channel_id=1, source_target_pairs={{0,1},{1,2},{2,3},{3,4},{4,5},{5,6},{6,7},{7,8},{8,9},{9,10},{10,1... | collective-permute-start | bytes 1544 | tf_op jit(solution)/shard_map/ppermute | solution.py:15
  2.7 29.0 %collective-permute-start.2 = (s32[128]{0:T(128)}, s32[128]{0:T(128)S(1)}, u32[]{:S(2)}, u32[]{:S(2)}) collective-permute-start(s32[128]{0:T(128)} %param.7), channel_id=1, source_target_pairs={{0,2},{1,3},{2,4},{3,5},{4,6},{5,7},{6,8},{7,9},{8,10},{9,11},{10,... | collective-permute-start | bytes 1544 | tf_op jit(solution)/shard_map/ppermute | solution.py:15
  7.2 30.2 %collective-permute-start.6 = (s32[128]{0:T(128)}, s32[128]{0:T(128)S(1)}, u32[]{:S(2)}, u32[]{:S(2)}) collective-permute-start(s32[128]{0:T(128)} %param.7), channel_id=1, source_target_pairs={{0,64},{32,96},{64,128},{96,160},{128,192},{160,224},{192,256},{22... | collective-permute-start | bytes 1544 | tf_op jit(solution)/shard_map/ppermute | solution.py:15
  13.3 26.1 %collective-permute-start.4 = (s32[128]{0:T(128)}, s32[128]{0:T(128)S(1)}, u32[]{:S(2)}, u32[]{:S(2)}) collective-permute-start(s32[128]{0:T(128)} %param.7), channel_id=1, source_target_pairs={{0,32},{32,64},{64,96},{96,128},{128,160},{160,192},{192,224},{224... | collective-permute-start | bytes 1544 | tf_op jit(solution)/shard_map/ppermute | solution.py:15
  19.8 64.0 %collective-permute-start.7 = (bf16[128,512]{0,1:T(8,128)(2,1)S(1)}, bf16[128,512]{0,1:T(8,128)(2,1)S(1)}, u32[]{:S(2)}, u32[]{:S(2)}) collective-permute-start(bf16[128,512]{0,1:T(8,128)(2,1)S(1)} %copy.25), channel_id=1, source_target_pairs={{0,64},{32,96},{64,128},{96,160},{128,192},{160,224},{192,256},{22... | collective-permute-start | bytes 393224 | tf_op jit(solution)/shard_map/ppermute | solution.py:15
  28.3 51.5 %collective-permute-start.5 = (bf16[128,512]{0,1:T(8,128)(2,1)S(1)}, bf16[128,512]{0,1:T(8,128)(2,1)S(1)}, u32[]{:S(2)}, u32[]{:S(2)}) collective-permute-start(bf16[128,512]{0,1:T(8,128)(2,1)S(1)} %copy.25), channel_id=1, source_target_pairs={{0,32},{32,64},{64,96},{96,128},{128,160},{160,192},{192,224},{224... | collective-permute-start | bytes 393224 | tf_op jit(solution)/shard_map/ppermute | solution.py:15
  31.7 28.3 %collective-permute-start.3 = (bf16[128,512]{0,1:T(8,128)(2,1)S(1)}, bf16[128,512]{0,1:T(8,128)(2,1)S(1)}, u32[]{:S(2)}, u32[]{:S(2)}) collective-permute-start(bf16[128,512]{0,1:T(8,128)(2,1)S(1)} %copy.25), channel_id=1, source_target_pairs={{0,2},{1,3},{2,4},{3,5},{4,6},{5,7},{6,8},{7,9},{8,10},{9,11},{10,... | collective-permute-start | bytes 393224 | tf_op jit(solution)/shard_map/ppermute | solution.py:15
  37.5 18.6 %collective-permute-start.1 = (bf16[128,512]{0,1:T(8,128)(2,1)S(1)}, bf16[128,512]{0,1:T(8,128)(2,1)S(1)}, u32[]{:S(2)}, u32[]{:S(2)}) collective-permute-start(bf16[128,512]{0,1:T(8,128)(2,1)S(1)} %copy.25), channel_id=1, source_target_pairs={{0,1},{1,2},{2,3},{3,4},{4,5},{5,6},{6,7},{7,8},{8,9},{9,10},{10,1... | collective-permute-start | bytes 393224 | tf_op jit(solution)/shard_map/ppermute | solution.py:15
  39.4 35.3 %collective-permute-start.9 = (bf16[128,512]{1,0:T(8,128)(2,1)S(1)}, bf16[128,512]{1,0:T(8,128)(2,1)S(1)}, u32[]{:S(2)}, u32[]{:S(2)}) collective-permute-start(bf16[128,512]{1,0:T(8,128)(2,1)S(1)} %copy-done.4), channel_id=1, source_target_pairs={{0,2},{1,3},{2,4},{3,5},{4,6},{5,7},{6,8},{7,9},{8,10},{9,11},{10,... | collective-permute-start | bytes 393224 | tf_op jit(solution)/shard_map/ppermute | solution.py:15
  56.0 11.5 %collective-permute-start.8 = (bf16[128,512]{1,0:T(8,128)(2,1)S(1)}, bf16[128,512]{1,0:T(8,128)(2,1)S(1)}, u32[]{:S(2)}, u32[]{:S(2)}) collective-permute-start(bf16[128,512]{1,0:T(8,128)(2,1)S(1)} %copy-done.4), channel_id=1, source_target_pairs={{0,1},{1,2},{2,3},{3,4},{4,5},{5,6},{6,7},{7,8},{8,9},{9,10},{10,1... | collective-permute-start | bytes 393224 | tf_op jit(solution)/shard_map/ppermute | solution.py:15
  60.0 5.9 %copy-start = (f32[4,128,128,16]{2,1,3,0:T(8,128)}, f32[4,128,128,16]{2,1,3,0:T(8,128)S(1)}, u32[]{:S(2)}) copy-start(f32[4,128,128,16]{2,1,3,0:T(8,128)S(1)} %get-tuple-element.25) | copy-start | bytes 12582916
  60.0 37.1 %collective-permute-start.11 = (bf16[128,512]{1,0:T(8,128)(2,1)S(1)}, bf16[128,512]{1,0:T(8,128)(2,1)S(1)}, u32[]{:S(2)}, u32[]{:S(2)}) collective-permute-start(bf16[128,512]{1,0:T(8,128)(2,1)S(1)} %copy-done.4), channel_id=1, source_target_pairs={{0,64},{32,96},{64,128},{96,160},{128,192},{160,224},{192,256},{22... | collective-permute-start | bytes 393224 | tf_op jit(solution)/shard_map/ppermute | solution.py:15
  63.4 2.5 %copy-start.1 = (f32[4,128,128,16]{2,1,3,0:T(8,128)}, f32[4,128,128,16]{2,1,3,0:T(8,128)S(1)}, u32[]{:S(2)}) copy-start(f32[4,128,128,16]{2,1,3,0:T(8,128)S(1)} %get-tuple-element.23) | copy-start | bytes 12582916
  67.5 20.2 %collective-permute-start.10 = (bf16[128,512]{1,0:T(8,128)(2,1)S(1)}, bf16[128,512]{1,0:T(8,128)(2,1)S(1)}, u32[]{:S(2)}, u32[]{:S(2)}) collective-permute-start(bf16[128,512]{1,0:T(8,128)(2,1)S(1)} %copy-done.4), channel_id=1, source_target_pairs={{0,32},{32,64},{64,96},{96,128},{128,160},{160,192},{192,224},{224... | collective-permute-start | bytes 393224 | tf_op jit(solution)/shard_map/ppermute | solution.py:15
  87.9 5.2 %copy-start.2 = (f32[4,128,128,16]{2,1,3,0:T(8,128)S(1)}, f32[4,128,128,16]{2,1,3,0:T(8,128)}, u32[]{:S(2)}) copy-start(f32[4,128,128,16]{2,1,3,0:T(8,128)} %get-tuple-element.21) | copy-start | bytes 12582916
  87.9 6.0 %copy-start.3 = (f32[4,128,128,16]{2,1,3,0:T(8,128)S(1)}, f32[4,128,128,16]{2,1,3,0:T(8,128)}, u32[]{:S(2)}) copy-start(f32[4,128,128,16]{2,1,3,0:T(8,128)} %get-tuple-element.29) | copy-start | bytes 12582916
where the time goes:
time: 110 us; the launch traced here: 109 us
  starting transfers between devices  41.4 us (38%)
  matrix products  41 us (37%)
  waiting for transfers between devices  9.36 us (9%)
  local copies, waits for them, and re-layouts  9.35 us (8%)
  other arithmetic  7.02 us (6%)
    ppermute x12, starting transfers between devices, from_behind(): return lax.ppermute(block, axis, route)  41.4 us
    dot_general x5, matrix products, block_terms(): jnp.einsum('kgtj,jkd->tkgd', weights, value_split, preferred_element_type...  27 us
    dot_general x5, matrix products, block_terms(): jnp.einsum('tkgd,jkd->kgtj', query_split, key_split, preferred_element_ty...  14 us
    ppermute x12, waiting for transfers between devices, from_behind(): return lax.ppermute(block, axis, route)  9.36 us
    unnamed x15, local copies, waits for them, and re-layouts  6.92 us
    reduce_sum x3, other arithmetic, block_terms(): total = jnp.sum(weights.astype(jnp.float32), axis=-1)  6.12 us
  transfers between devices with their start and end apart: 12, of which 2 were waited for; matrix products, arithmetic and copies ran while one was open for 41% of the time, Pallas kernels for 0%

commit v1 on v0

v1 whole, which is shorter than its diff:
```python
import functools
import math

import jax
import jax.numpy as jnp
from jax import lax
from jax.experimental import pallas as pl
from jax.experimental.pallas import tpu as pltpu
from jax.sharding import PartitionSpec as P

MESH = pl.DeviceIdType.MESH
WIDTH = 128
KV = 4
GROUP = 16
STACK = 4
STEPS = KV * GROUP // STACK
PER = GROUP // STACK
HIDE = -65536.0
SCALE = 1.0 / math.sqrt(WIDTH)
SCALE2 = SCALE * math.log2(math.e)
VMEM = 60 * 2**20
ABSENT = 4.0
ROWS = 2 * WIDTH + 16

OWN, NEAR, SECOND, FAR, DISTANT = range(5)


def nt(a, b):
    return lax.dot_general(a, b, (((1,), (1,)), ((), ())), preferred_element_type=jnp.float32)


def kernel(
    n_outer, n_inner, q_hbm, k_hbm, v_hbm, doc_hbm, o_hbm, log_ref,
    queries, result, got, seen_by, marks, peaks, totals, scores, weights,
    doc_ref, stage_sem, q_sem, o_sem, doc_sem, send_sem, recv_sem,
):
    outer, inner = lax.axis_index("outer"), lax.axis_index("inner")
    core = lax.rem(inner, 2)
    place = outer * n_inner + inner
    count = n_outer * n_inner

    def device(where):
        where = jnp.clip(where, 0, count - 1)
        return (where // n_inner, lax.rem(where, n_inner))

    has_far, gives_far = outer >= 1, outer < n_outer - 1
    has_distant = outer >= 2
    has_second, gives_second = place >= 2, place + 2 < count
    partner = (outer, inner + 1 - 2 * core)
    ahead = (jnp.minimum(outer + 1, n_outer - 1), inner)
    behind = (jnp.maximum(outer - 1, 0), inner)

    doc_copy = pltpu.make_async_copy(doc_hbm, doc_ref, doc_sem)
    doc_copy.start()
    staged = []
    for g in range(KV):
        for i, ref in enumerate((k_hbm, v_hbm)):
            copy = pltpu.make_async_copy(
                ref.at[:, pl.ds(g * WIDTH, WIDTH)],
                got.at[OWN, g, pl.ds(i * WIDTH, WIDTH)],
                stage_sem.at[g, i],
            )
            copy.start()
            staged.append(copy)
    fetch = []
    wide = GROUP * WIDTH
    for g in range(KV):
        copy = pltpu.make_async_copy(
            q_hbm.at[:, pl.ds(g * wide, wide)], queries.at[:, pl.ds(g * wide, wide)], q_sem.at[g]
        )
        copy.start()
        fetch.append(copy)

    barrier = pltpu.get_barrier_semaphore()

    @pl.when(has_far)
    def _():
        pl.semaphore_signal(barrier, inc=1, device_id=behind, device_id_type=MESH)

    @pl.when(has_second)
    def _():
        pl.semaphore_signal(barrier, inc=1, device_id=device(place - 2), device_id_type=MESH)

    pl.semaphore_signal(barrier, inc=1, device_id=partner, device_id_type=MESH)

    doc_copy.wait()
    docs = doc_ref[...].astype(jnp.float32)
    got[OWN, 0, pl.ds(2 * WIDTH, 16)] = jnp.broadcast_to(docs, (16, WIDTH)).astype(jnp.bfloat16)

    for slot, absent in (
        (NEAR, place < 1), (SECOND, place < 2), (FAR, outer < 1), (DISTANT, outer < 2),
    ):

        @pl.when(absent)
        def _(slot=slot):
            got[slot] = jnp.zeros((KV, ROWS, WIDTH), jnp.bfloat16)
            got[slot, 0, pl.ds(2 * WIDTH, 16)] = jnp.full((16, WIDTH), ABSENT, jnp.bfloat16)

    def copy_of(kind, g, source, target):
        rows = pl.ds(0, ROWS if g == 0 else 2 * WIDTH)
        return pltpu.make_async_remote_copy(
            src_ref=got.at[source, g, rows],
            dst_ref=got.at[kind, g, rows],
            send_sem=send_sem.at[kind - 1, g],
            recv_sem=recv_sem.at[kind - 1, g],
            device_id=target,
            device_id_type=MESH,
        )

    def far(g):
        return copy_of(FAR, g, OWN, ahead)

    def distant(g):
        return copy_of(DISTANT, g, FAR, ahead)

    def second(g):
        return copy_of(SECOND, g, OWN, device(place + 2))

    def near(g):
        return copy_of(NEAR, g, OWN, partner)

    def near_back(g):
        return copy_of(NEAR, g, SECOND, partner)

    def on(condition, act):
        @pl.when(condition)
        def _():
            act()

    def send_own(g):
        on(gives_far, lambda: far(g).start())
        on(gives_second, lambda: second(g).start())
        on(core == 0, lambda: near(g).start())

    def pass_on(g):
        on(has_far, lambda: far(g).wait_recv())
        on(has_far & gives_far, lambda: distant(g).start())
        on(has_second, lambda: second(g).wait_recv())
        on((core == 1) & has_second, lambda: near_back(g).start())

    def arrive(g):
        on(has_distant, lambda: distant(g).wait_recv())
        on((core == 1) | has_second, lambda: near(g).wait_recv())

    for copy in staged[:4]:
        copy.wait()

    pl.semaphore_wait(barrier, 1 + gives_far.astype(jnp.int32) + gives_second.astype(jnp.int32))

    send_own(0)
    send_own(1)
    for copy in staged[4:]:
        copy.wait()

    lane = lax.broadcasted_iota(jnp.int32, (WIDTH, WIDTH), 1)
    row = lax.broadcasted_iota(jnp.int32, (WIDTH, WIDTH), 0)
    lane_f = lane.astype(jnp.float32)
    mine = jnp.broadcast_to(docs, (WIDTH, WIDTH))
    mine_down = mine.T
    marks[0] = jnp.where((lane > row) | (mine != mine_down), HIDE, 0.0).astype(jnp.bfloat16)
    marks[1] = jnp.where(lane_f != mine_down, HIDE, 0.0).astype(jnp.bfloat16)
    seen_by[OWN] = jnp.where(lane == row, 1.0, 0.0).astype(jnp.bfloat16)

    def note_documents():
        for slot in (NEAR, SECOND, FAR, DISTANT):
            theirs = got[slot, 0, pl.ds(2 * WIDTH, 16)].astype(jnp.float32)[0:1]
            down = jnp.broadcast_to(theirs, (WIDTH, WIDTH)).T
            seen_by[slot] = jnp.where(lane_f == down, 1.0, 0.0).astype(jnp.bfloat16)

    ones = jnp.ones((WIDTH, WIDTH), jnp.bfloat16)

    def columns(it, i):
        return pl.ds((it * STACK + i) * WIDTH, WIDTH)

    def multiply_keys(it):
        g, slot = it // PER, it % 2
        heads = [queries[:, columns(it, i)] for i in range(STACK)]
        own_side, far_side = (
            jnp.concatenate([jnp.concatenate([q, marks[k]], axis=1) for q in heads], axis=0)
            for k in range(2)
        )

        def key_side(block):
            return jnp.concatenate([got[block, g, pl.ds(0, WIDTH)], seen_by[block]], axis=1)

        scores[slot, :, 0:128] = nt(own_side, key_side(OWN))
        scores[slot, :, 128:384] = nt(
            far_side, jnp.concatenate([key_side(NEAR), key_side(SECOND)], axis=0)
        )
        scores[slot, :, 384:640] = nt(
            far_side, jnp.concatenate([key_side(FAR), key_side(DISTANT)], axis=0)
        )

    def weigh(it):
        slot = it % 2
        for i in range(STACK):
            rows = pl.ds(i * WIDTH, WIDTH)
            s = scores[slot, rows]
            peak = jnp.max(s, axis=1, keepdims=True)
            weights[slot, rows] = jnp.exp2((s - peak) * SCALE2).astype(jnp.bfloat16)
            peaks[...] = jnp.where(lane == it * STACK + i, peak, peaks[...])

    def multiply_values(it):
        g, slot = it // PER, it % 2
        value_side = jnp.concatenate(
            [
                jnp.concatenate([got[block, g, pl.ds(WIDTH, WIDTH)], ones], axis=1)
                for block in range(5)
            ],
            axis=0,
        )
        sums = jnp.dot(weights[slot], value_side, preferred_element_type=jnp.float32)
        for i in range(STACK):
            part = sums[i * WIDTH : (i + 1) * WIDTH]
            total = part[:, WIDTH:]
            result[:, columns(it, i)] = (part[:, :WIDTH] / total).astype(jnp.bfloat16)
            totals[...] = jnp.where(lane == it * STACK + i, total, totals[...])

    def put(g):
        return pltpu.make_async_copy(
            result.at[:, pl.ds(g * wide, wide)], o_hbm.at[:, pl.ds(g * wide, wide)], o_sem.at[g]
        )

    peaks[...] = jnp.zeros_like(peaks)
    totals[...] = jnp.ones_like(totals)
    for it in range(STEPS + 2):
        g = it // PER
        if it < STEPS and it % PER == 0:
            if g == 0:
                pass_on(0)
                send_own(2)
                pass_on(1)
                send_own(3)
            if g + 2 < KV:
                pass
            arrive(g)
            if g == 0:
                note_documents()
            fetch[g].wait()
        if it == PER // 2:
            pass_on(2)
        if it == PER + PER // 2:
            pass_on(3)
        if it >= 2:
            multiply_values(it - 2)
            if (it - 2) % PER == PER - 1:
                put((it - 2) // PER).start()
        if it < STEPS:
            multiply_keys(it)
        if 1 <= it <= STEPS:
            weigh(it - 1)

    log_norm = peaks[...] * SCALE + jnp.log(totals[...])
    log_ref[...] = log_norm.T[0 : KV * GROUP]
    for g in range(KV):
        put(g).wait()
        on(gives_far, lambda: far(g).wait_send())
        on(has_far & gives_far, lambda: distant(g).wait_send())
        on(gives_second, lambda: second(g).wait_send())
        on((core == 0) | has_second, lambda: near(g).wait_send())


def on_device(queries, keys, values, doc_ids):
    block, width = queries.shape
    n_outer, n_inner = lax.axis_size("outer"), lax.axis_size("inner")
    anywhere = pl.BlockSpec(memory_space=pl.ANY)
    vmem = pl.BlockSpec(memory_space=pltpu.VMEM)
    square = (WIDTH, WIDTH)
    return pl.pallas_call(
        functools.partial(kernel, n_outer, n_inner),
        out_shape=(
            jax.ShapeDtypeStruct((block, width), jnp.bfloat16),
            jax.ShapeDtypeStruct((KV * GROUP, block), jnp.float32),
        ),
        in_specs=[anywhere] * 4,
        out_specs=(anywhere, vmem),
        scratch_shapes=[
            pltpu.VMEM((block, width), jnp.bfloat16),
            pltpu.VMEM((block, width), jnp.bfloat16),
            pltpu.VMEM((5, KV, ROWS, WIDTH), jnp.bfloat16),
            pltpu.VMEM((5,) + square, jnp.bfloat16),
            pltpu.VMEM((2,) + square, jnp.bfloat16),
            pltpu.VMEM(square, jnp.float32),
            pltpu.VMEM(square, jnp.float32),
            pltpu.VMEM((2, STACK * WIDTH, 5 * WIDTH), jnp.float32),
            pltpu.VMEM((2, STACK * WIDTH, 5 * WIDTH), jnp.bfloat16),
            pltpu.VMEM((1, WIDTH), jnp.int32),
            pltpu.SemaphoreType.DMA((KV, 2)),
            pltpu.SemaphoreType.DMA((KV,)),
            pltpu.SemaphoreType.DMA((KV,)),
            pltpu.SemaphoreType.DMA,
            pltpu.SemaphoreType.DMA((4, KV)),
            pltpu.SemaphoreType.DMA((4, KV)),
        ],
        compiler_params=pltpu.CompilerParams(
            collective_id=0, has_side_effects=True, vmem_limit_bytes=VMEM
        ),
        name="attention",
    )(queries, keys, values, doc_ids.reshape(1, block))


def solution(mesh):
    split = ("outer", "inner")
    return jax.shard_map(
        on_device,
        mesh=mesh,
        in_specs=(P(split, None), P(split, None), P(split, None), P(split)),
        out_specs=(P(split, None), P(None, split)),
        check_vma=False,
    )
```

time: 110 us -> 50.4 us (0.46)
  the two profiles are of different devices: /device:TPU:64 before, /device:TPU:8 now
where the time goes in v1:
time: 50.4 us; the launch traced here: 50.2 us
  Pallas kernels  45.8 us (91%)
  local copies, waits for them, and re-layouts  3.72 us (7%)
  between operations  0.65 us (1%)
    pallas_call x1, Pallas kernels, on_device(): pl.pallas_call(functools.partial(kernel, n_outer, n_inner), out_shape=(ja...  45.8 us
    unnamed x4, local copies, waits for them, and re-layouts  3.72 us

profile of v1, /device:TPU:8, one launch (start us, length us, event | category | flops | bytes accessed | tf_op | source)
XLA Modules:
  0.0 50.2 jit_solution(14154491565845188130)
XLA Ops:
  0.6 45.8 %attention.1 = (bf16[128,8192]{1,0:T(8,128)(2,1)}, f32[64,128]{1,0:T(8,128)}) custom-call(bf16[128,8192]{1,0:T(8,128)(2,1)} %q_hbm.1, bf16[128,512]{1,0:T(8,128)(2,1)} %k_hbm.1, bf16[128,512]{1,0:T(8,128)(2,1)} %v_hbm.1, s32[1,128]{1,0:T(1,128)} %bitcast.1), custom_call_target="tpu_custom_call" | custom-call | tf_op jit(solution)/shard_map/attention/pallas_call | solution.py:269
  46.5 0.0 copy-start
  46.5 3.1 %copy.8 = bf16[128,8192]{1,0:T(8,128)(2,1)} copy(bf16[128,8192]{1,0:T(8,128)(2,1)} %get-tuple-element.4) | data formatting | bytes 4194304
  49.6 0.0 copy-done
  49.6 0.6 %copy.9 = f32[64,128]{1,0:T(8,128)} copy(f32[64,128]{1,0:T(8,128)S(1)} %copy-done) | data formatting | bytes 65536
Async XLA Ops:
  46.5 3.1 %copy-start = (f32[64,128]{1,0:T(8,128)S(1)}, f32[64,128]{1,0:T(8,128)}, u32[]{:S(2)}) copy-start(f32[64,128]{1,0:T(8,128)} %get-tuple-element.5) | copy-start | bytes 98308

commit v2 on v1

--- a/solution.py
+++ b/solution.py
@@ -18,8 +18,17 @@
 HIDE = -65536.0
 SCALE = 1.0 / math.sqrt(WIDTH)
 SCALE2 = SCALE * math.log2(math.e)
-VMEM = 60 * 2**20
+VMEM = 58 * 2**20
 ABSENT = 4.0
+PLAN = {step: "" for step in range(STEPS + 3)} | {
+    0: "L0 F0 S0 N0 L1 F1 S1 N1 L2 L3",
+    1: "D0 F2 S2 N2 B0 D1 F3 S3 N3 B1 A0",
+    3: "D2 B2",
+    5: "A1",
+    7: "D3 B3",
+    9: "A2",
+    13: "A3",
+}
 ROWS = 2 * WIDTH + 16
 
 OWN, NEAR, SECOND, FAR, DISTANT = range(5)
@@ -30,9 +39,9 @@
 
 
 def kernel(
-    n_outer, n_inner, q_hbm, k_hbm, v_hbm, doc_hbm, o_hbm, log_ref,
-    queries, result, got, seen_by, marks, peaks, totals, scores, weights,
-    doc_ref, stage_sem, q_sem, o_sem, doc_sem, send_sem, recv_sem,
+    n_outer, n_inner, q_hbm, k_hbm, v_hbm, doc_hbm, result, log_ref,
+    queries, got, seen_by, marks, peaks, totals, scores, weights,
+    doc_ref, stage_sem, q_sem, doc_sem, send_sem, recv_sem,
 ):
     outer, inner = lax.axis_index("outer"), lax.axis_index("inner")
     core = lax.rem(inner, 2)
@@ -127,30 +136,37 @@
         def _():
             act()
 
-    def send_own(g):
-        on(gives_far, lambda: far(g).start())
-        on(gives_second, lambda: second(g).start())
-        on(core == 0, lambda: near(g).start())
-
-    def pass_on(g):
-        on(has_far, lambda: far(g).wait_recv())
-        on(has_far & gives_far, lambda: distant(g).start())
-        on(has_second, lambda: second(g).wait_recv())
-        on((core == 1) & has_second, lambda: near_back(g).start())
-
-    def arrive(g):
-        on(has_distant, lambda: distant(g).wait_recv())
-        on((core == 1) | has_second, lambda: near(g).wait_recv())
-
-    for copy in staged[:4]:
-        copy.wait()
+    def do(word):
+        what, g = word[0], int(word[1])
+        if what == "L":
+            for copy in staged[2 * g : 2 * g + 2]:
+                copy.wait()
+        elif what == "F":
+            on(gives_far, lambda: far(g).start())
+        elif what == "S":
+            on(gives_second, lambda: second(g).start())
+        elif what == "N":
+            on(core == 0, lambda: near(g).start())
+        elif what == "D":
+            on(has_far, lambda: far(g).wait_recv())
+            on(has_far & gives_far, lambda: distant(g).start())
+        elif what == "B":
+            on(has_second, lambda: second(g).wait_recv())
+            on((core == 1) & has_second, lambda: near_back(g).start())
+        elif what == "A":
+            on(has_distant, lambda: distant(g).wait_recv())
+            on((core == 1) | has_second, lambda: near(g).wait_recv())
+            if g == 0:
+                note_documents()
+            fetch[g].wait()
+
+    def run_plan(plan):
+        for word in plan.split():
+            do(word)
 
     pl.semaphore_wait(barrier, 1 + gives_far.astype(jnp.int32) + gives_second.astype(jnp.int32))
 
-    send_own(0)
-    send_own(1)
-    for copy in staged[4:]:
-        copy.wait()
+    run_plan(PLAN[0])
 
     lane = lax.broadcasted_iota(jnp.int32, (WIDTH, WIDTH), 1)
     row = lax.broadcasted_iota(jnp.int32, (WIDTH, WIDTH), 0)
@@ -216,35 +232,12 @@
             result[:, columns(it, i)] = (part[:, :WIDTH] / total).astype(jnp.bfloat16)
             totals[...] = jnp.where(lane == it * STACK + i, total, totals[...])
 
-    def put(g):
-        return pltpu.make_async_copy(
-            result.at[:, pl.ds(g * wide, wide)], o_hbm.at[:, pl.ds(g * wide, wide)], o_sem.at[g]
-        )
-
     peaks[...] = jnp.zeros_like(peaks)
     totals[...] = jnp.ones_like(totals)
     for it in range(STEPS + 2):
-        g = it // PER
-        if it < STEPS and it % PER == 0:
-            if g == 0:
-                pass_on(0)
-                send_own(2)
-                pass_on(1)
-                send_own(3)
-            if g + 2 < KV:
-                pass
-            arrive(g)
-            if g == 0:
-                note_documents()
-            fetch[g].wait()
-        if it == PER // 2:
-            pass_on(2)
-        if it == PER + PER // 2:
-            pass_on(3)
+        run_plan(PLAN[it + 1])
         if it >= 2:
             multiply_values(it - 2)
-            if (it - 2) % PER == PER - 1:
-                put((it - 2) // PER).start()
         if it < STEPS:
             multiply_keys(it)
         if 1 <= it <= STEPS:
@@ -253,7 +246,6 @@
     log_norm = peaks[...] * SCALE + jnp.log(totals[...])
     log_ref[...] = log_norm.T[0 : KV * GROUP]
     for g in range(KV):
-        put(g).wait()
         on(gives_far, lambda: far(g).wait_send())
         on(has_far & gives_far, lambda: distant(g).wait_send())
         on(gives_second, lambda: second(g).wait_send())
@@ -269,13 +261,12 @@
     return pl.pallas_call(
         functools.partial(kernel, n_outer, n_inner),
         out_shape=(
-            jax.ShapeDtypeStruct((block, width), jnp.bfloat16),
-            jax.ShapeDtypeStruct((KV * GROUP, block), jnp.float32),
+            pltpu.VMEM((block, width), jnp.bfloat16),
+            pltpu.VMEM((KV * GROUP, block), jnp.float32),
         ),
         in_specs=[anywhere] * 4,
-        out_specs=(anywhere, vmem),
+        out_specs=(vmem, vmem),
         scratch_shapes=[
-            pltpu.VMEM((block, width), jnp.bfloat16),
             pltpu.VMEM((block, width), jnp.bfloat16),
             pltpu.VMEM((5, KV, ROWS, WIDTH), jnp.bfloat16),
             pltpu.VMEM((5,) + square, jnp.bfloat16),
@@ -287,7 +278,6 @@
             pltpu.VMEM((1, WIDTH), jnp.int32),
             pltpu.SemaphoreType.DMA((KV, 2)),
             pltpu.SemaphoreType.DMA((KV,)),
-            pltpu.SemaphoreType.DMA((KV,)),
             pltpu.SemaphoreType.DMA,
             pltpu.SemaphoreType.DMA((4, KV)),
             pltpu.SemaphoreType.DMA((4, KV)),

time: 50.4 us -> 47.2 us (0.937)
  local copies, waits for them, and re-layouts: 3.72 us -> 1.94 us
  Pallas kernels: 45.8 us -> 44.5 us
    unnamed x4 -> x2, local copies, waits for them, and re-layouts: 3.72 us -> 1.94 us
    pallas_call x1, Pallas kernels: 45.8 us -> 44.5 us  [on_device(): pl.pallas_call(functools.partial(kernel, n_outer, n_inner), out_shape=(pl...]
where the time goes in v2:
time: 47.2 us; the launch traced here: 47.1 us
  Pallas kernels  44.5 us (94%)
  local copies, waits for them, and re-layouts  1.94 us (4%)
  between operations  0.64 us (1%)
    pallas_call x1, Pallas kernels, on_device(): pl.pallas_call(functools.partial(kernel, n_outer, n_inner), out_shape=(pl...  44.5 us
    unnamed x2, local copies, waits for them, and re-layouts  1.94 us

profile of v2, /device:TPU:8, one launch (start us, length us, event | category | flops | bytes accessed | tf_op | source)
XLA Modules:
  0.0 47.1 jit_solution(5783427832009295357)
XLA Ops:
  0.6 44.5 %attention.1 = (bf16[128,8192]{1,0:T(8,128)(2,1)S(1)}, f32[64,128]{1,0:T(8,128)S(1)}) custom-call(bf16[128,8192]{1,0:T(8,128)(2,1)} %q_hbm.1, bf16[128,512]{1,0:T(8,128)(2,1)} %k_hbm.1, bf16[128,512]{1,0:T(8,128)(2,1)} %v_hbm.1, s32[1,128]{1,0:T(1,128)} %bitcast.1), custom_call_target="tpu_custom_call" | custom-call | tf_op jit(solution)/shard_map/attention/pallas_call | solution.py:261
  45.1 1.3 %copy.8 = bf16[128,8192]{1,0:T(8,128)(2,1)} copy(bf16[128,8192]{1,0:T(8,128)(2,1)S(1)} %get-tuple-element.2) | data formatting | bytes 4194304
  46.4 0.6 %copy.9 = f32[64,128]{1,0:T(8,128)} copy(f32[64,128]{1,0:T(8,128)S(1)} %get-tuple-element.3) | data formatting | bytes 65536

commit v3 on v2

--- a/solution.py
+++ b/solution.py
@@ -21,17 +21,19 @@
 VMEM = 58 * 2**20
 ABSENT = 4.0
 PLAN = {step: "" for step in range(STEPS + 3)} | {
-    0: "L0 F0 S0 N0 L1 F1 S1 N1 L2 L3",
-    1: "D0 F2 S2 N2 B0 D1 F3 S3 N3 B1 A0",
-    3: "D2 B2",
-    5: "A1",
-    7: "D3 B3",
-    9: "A2",
-    13: "A3",
+    0: "L0 L1 L2 L3 T0 T1 T2 T3 E0 E1 E2 E3 F0 S0 N0 F1 S1 N1 S2 N2 S3 N3",
+    1: "x0 x1 x2 x3 W0 G0 G1 G2 G3 d0 d1 d2 d3 D0 F2 D1 F3 B0 B1 w0 g0 g1 g2 g3 A0 Q0 Q1",
+    3: "D2 B2 Q2",
+    5: "A1 Q3",
+    7: "D3 B3 R0",
+    9: "A2 R1",
+    11: "R2",
+    13: "A3 R3",
 }
 ROWS = 2 * WIDTH + 16
 
-OWN, NEAR, SECOND, FAR, DISTANT = range(5)
+OWN, NEAR, SECOND, FAR, DISTANT, PASSING, CROSSING = range(7)
+RELAYED = (1, 2, 3)
 
 
 def nt(a, b):
@@ -41,7 +43,7 @@
 def kernel(
     n_outer, n_inner, q_hbm, k_hbm, v_hbm, doc_hbm, result, log_ref,
     queries, got, seen_by, marks, peaks, totals, scores, weights,
-    doc_ref, stage_sem, q_sem, doc_sem, send_sem, recv_sem,
+    doc_ref, stage_sem, q_sem, doc_sem, send_sem, recv_sem, ready,
 ):
     outer, inner = lax.axis_index("outer"), lax.axis_index("inner")
     core = lax.rem(inner, 2)
@@ -56,6 +58,12 @@
     has_distant = outer >= 2
     has_second, gives_second = place >= 2, place + 2 < count
     partner = (outer, inner + 1 - 2 * core)
+    half = n_outer // 2
+    opens = lax.rem(outer, half) == 0
+    follows = lax.rem(outer, half) == 1
+    before, middle, relay = outer == half - 1, outer == half, outer == 0
+    late = (outer >= half - 1) & (outer <= half + 2)
+    hurried = (late & ~middle) | (outer == half - 2)
     ahead = (jnp.minimum(outer + 1, n_outer - 1), inner)
     behind = (jnp.maximum(outer - 1, 0), inner)
 
@@ -82,15 +90,17 @@
 
     barrier = pltpu.get_barrier_semaphore()
 
-    @pl.when(has_far)
-    def _():
-        pl.semaphore_signal(barrier, inc=1, device_id=behind, device_id_type=MESH)
-
-    @pl.when(has_second)
-    def _():
-        pl.semaphore_signal(barrier, inc=1, device_id=device(place - 2), device_id_type=MESH)
-
-    pl.semaphore_signal(barrier, inc=1, device_id=partner, device_id_type=MESH)
+    def greet(condition, target, semaphore=barrier):
+        @pl.when(condition)
+        def _():
+            pl.semaphore_signal(semaphore, inc=1, device_id=target, device_id_type=MESH)
+
+    greet(has_far & ~follows, behind)
+    greet(opens, ahead)
+    greet(relay, (half - 1, inner))
+    greet(middle, (0, inner))
+    greet(has_second, device(place - 2))
+    greet(place >= 0, partner)
 
     doc_copy.wait()
     docs = doc_ref[...].astype(jnp.float32)
@@ -105,13 +115,13 @@
             got[slot] = jnp.zeros((KV, ROWS, WIDTH), jnp.bfloat16)
             got[slot, 0, pl.ds(2 * WIDTH, 16)] = jnp.full((16, WIDTH), ABSENT, jnp.bfloat16)
 
-    def copy_of(kind, g, source, target):
+    def copy_of(kind, g, source, target, landing=None):
         rows = pl.ds(0, ROWS if g == 0 else 2 * WIDTH)
         return pltpu.make_async_remote_copy(
             src_ref=got.at[source, g, rows],
-            dst_ref=got.at[kind, g, rows],
+            dst_ref=got.at[landing or kind, g, rows],
             send_sem=send_sem.at[kind - 1, g],
-            recv_sem=recv_sem.at[kind - 1, g],
+            recv_sem=recv_sem.at[(landing or kind) - 1, g],
             device_id=target,
             device_id_type=MESH,
         )
@@ -121,6 +131,18 @@
 
     def distant(g):
         return copy_of(DISTANT, g, FAR, ahead)
+
+    def to_relay(g):
+        return copy_of(DISTANT, g, FAR, (0, inner), PASSING)
+
+    def from_relay(g):
+        return copy_of(DISTANT, g, PASSING, (half, inner))
+
+    def to_crossing(g):
+        return copy_of(FAR, g, OWN, (0, inner), CROSSING)
+
+    def from_crossing(g):
+        return copy_of(PASSING, g, CROSSING, (half, inner), FAR)
 
     def second(g):
         return copy_of(SECOND, g, OWN, device(place + 2))
@@ -135,21 +157,43 @@
         @pl.when(condition)
         def _():
             act()
+
+    turns = before & (inner >= n_inner - 2)
+
+    def crosses(g):
+        return (inner >= 0) if g in RELAYED else (inner < 2)
 
     def do(word):
         what, g = word[0], int(word[1])
         if what == "L":
             for copy in staged[2 * g : 2 * g + 2]:
                 copy.wait()
+        elif what == "E":
+            on(before & crosses(g), lambda: to_crossing(g).start())
+            on(hurried & ~(before & crosses(g)), lambda: far(g).start())
+        elif what == "T":
+            on(turns, lambda: second(g).start())
         elif what == "F":
-            on(gives_far, lambda: far(g).start())
+            on(gives_far & ~hurried & ~opens, lambda: far(g).start())
+        elif what in "Ww":
+            on(middle if what == "W" else relay, lambda: pl.semaphore_wait(ready, 1))
+        elif what in "Gg":
+            on(middle if what == "G" else relay, lambda: far(g).start())
+        elif what == "Q":
+            on(relay & crosses(g), lambda: to_crossing(g).wait_recv())
+            on(relay & crosses(g), lambda: from_crossing(g).start())
+        elif what == "R":
+            on(relay, lambda: to_relay(g).wait_recv())
+            on(relay, lambda: from_relay(g).start())
         elif what == "S":
-            on(gives_second, lambda: second(g).start())
+            on(gives_second & ~turns, lambda: second(g).start())
         elif what == "N":
             on(core == 0, lambda: near(g).start())
-        elif what == "D":
-            on(has_far, lambda: far(g).wait_recv())
-            on(has_far & gives_far, lambda: distant(g).start())
+        elif what in "Ddx":
+            now = {"D": ~late | middle, "d": late & ~before & ~middle, "x": before}[what]
+            on(now & has_far, lambda: far(g).wait_recv())
+            on(now & has_far & gives_far & ~before, lambda: distant(g).start())
+            on(now & before, lambda: to_relay(g).start())
         elif what == "B":
             on(has_second, lambda: second(g).wait_recv())
             on((core == 1) & has_second, lambda: near_back(g).start())
@@ -164,7 +208,11 @@
         for word in plan.split():
             do(word)
 
-    pl.semaphore_wait(barrier, 1 + gives_far.astype(jnp.int32) + gives_second.astype(jnp.int32))
+    peers = 1
+    for peer in (gives_far & ~opens, follows, before, relay, gives_second):
+        peers = peers + peer.astype(jnp.int32)
+    pl.semaphore_wait(barrier, peers)
+    greet(follows, behind, ready)
 
     run_plan(PLAN[0])
 
@@ -247,7 +295,8 @@
     log_ref[...] = log_norm.T[0 : KV * GROUP]
     for g in range(KV):
         on(gives_far, lambda: far(g).wait_send())
-        on(has_far & gives_far, lambda: distant(g).wait_send())
+        on((has_far & gives_far) | relay, lambda: distant(g).wait_send())
+        on(relay & crosses(g), lambda: from_crossing(g).wait_send())
         on(gives_second, lambda: second(g).wait_send())
         on((core == 0) | has_second, lambda: near(g).wait_send())
 
@@ -268,7 +317,7 @@
         out_specs=(vmem, vmem),
         scratch_shapes=[
             pltpu.VMEM((block, width), jnp.bfloat16),
-            pltpu.VMEM((5, KV, ROWS, WIDTH), jnp.bfloat16),
+            pltpu.VMEM((7, KV, ROWS, WIDTH), jnp.bfloat16),
             pltpu.VMEM((5,) + square, jnp.bfloat16),
             pltpu.VMEM((2,) + square, jnp.bfloat16),
             pltpu.VMEM(square, jnp.float32),
@@ -279,8 +328,9 @@
             pltpu.SemaphoreType.DMA((KV, 2)),
             pltpu.SemaphoreType.DMA((KV,)),
             pltpu.SemaphoreType.DMA,
-            pltpu.SemaphoreType.DMA((4, KV)),
-            pltpu.SemaphoreType.DMA((4, KV)),
+            pltpu.SemaphoreType.DMA((5, KV)),
+            pltpu.SemaphoreType.DMA((6, KV)),
+            pltpu.SemaphoreType.REGULAR,
         ],
         compiler_params=pltpu.CompilerParams(
             collective_id=0, has_side_effects=True, vmem_limit_bytes=VMEM

time: 47.2 us -> 40.1 us (0.85)
  the two profiles are of different devices: /device:TPU:8 before, /device:TPU:126 now
where the time goes in v3:
time: 40.1 us; the launch traced here: 40 us
  Pallas kernels  37.4 us (93%)
  local copies, waits for them, and re-layouts  1.94 us (5%)
  between operations  0.64 us (2%)
    pallas_call x1, Pallas kernels, on_device(): pl.pallas_call(functools.partial(kernel, n_outer, n_inner), out_shape=(pl...  37.4 us
    unnamed x2, local copies, waits for them, and re-layouts  1.94 us

profile of v3, /device:TPU:126, one launch (start us, length us, event | category | flops | bytes accessed | tf_op | source)
XLA Modules:
  0.0 40.0 jit_solution(4533731046163597063)
XLA Ops:
  0.6 37.4 %attention.1 = (bf16[128,8192]{1,0:T(8,128)(2,1)S(1)}, f32[64,128]{1,0:T(8,128)S(1)}) custom-call(bf16[128,8192]{1,0:T(8,128)(2,1)} %q_hbm.1, bf16[128,512]{1,0:T(8,128)(2,1)} %k_hbm.1, bf16[128,512]{1,0:T(8,128)(2,1)} %v_hbm.1, s32[1,128]{1,0:T(1,128)} %bitcast.1), custom_call_target="tpu_custom_call" | custom-call | tf_op jit(solution)/shard_map/attention/pallas_call | solution.py:310
  38.0 1.3 %copy.8 = bf16[128,8192]{1,0:T(8,128)(2,1)} copy(bf16[128,8192]{1,0:T(8,128)(2,1)S(1)} %get-tuple-element.2) | data formatting | bytes 4194304
  39.4 0.6 %copy.9 = f32[64,128]{1,0:T(8,128)} copy(f32[64,128]{1,0:T(8,128)S(1)} %get-tuple-element.3) | data formatting | bytes 65536

commit v4 on v3

--- a/solution.py
+++ b/solution.py
@@ -22,7 +22,7 @@
 ABSENT = 4.0
 PLAN = {step: "" for step in range(STEPS + 3)} | {
     0: "L0 L1 L2 L3 T0 T1 T2 T3 E0 E1 E2 E3 F0 S0 N0 F1 S1 N1 S2 N2 S3 N3",
-    1: "x0 x1 x2 x3 W0 G0 G1 G2 G3 d0 d1 d2 d3 D0 F2 D1 F3 B0 B1 w0 g0 g1 g2 g3 A0 Q0 Q1",
+    1: "x0 x1 x2 x3 W0 G0 G1 G2 G3 d0 d1 d2 d3 D0 F2 D1 F3 B0 B1 w0 g0 g1 g2 g3 Q0 Q1 A0",
     3: "D2 B2 Q2",
     5: "A1 Q3",
     7: "D3 B3 R0",
@@ -33,7 +33,7 @@
 ROWS = 2 * WIDTH + 16
 
 OWN, NEAR, SECOND, FAR, DISTANT, PASSING, CROSSING = range(7)
-RELAYED = (1, 2, 3)
+RELAYED = (0, 1, 2, 3)
 
 
 def nt(a, b):

time: 40.1 us -> 39 us (0.973)
  the two profiles are of different devices: /device:TPU:126 before, /device:TPU:8 now
where the time goes in v4:
time: 39 us; the launch traced here: 38.9 us
  Pallas kernels  36.3 us (93%)
  local copies, waits for them, and re-layouts  1.94 us (5%)
  between operations  0.64 us (2%)
    pallas_call x1, Pallas kernels, on_device(): pl.pallas_call(functools.partial(kernel, n_outer, n_inner), out_shape=(pl...  36.3 us
    unnamed x2, local copies, waits for them, and re-layouts  1.94 us

profile of v4, /device:TPU:8, one launch (start us, length us, event | category | flops | bytes accessed | tf_op | source)
XLA Modules:
  0.0 38.9 jit_solution(12783110527045267274)
XLA Ops:
  0.6 36.3 %attention.1 = (bf16[128,8192]{1,0:T(8,128)(2,1)S(1)}, f32[64,128]{1,0:T(8,128)S(1)}) custom-call(bf16[128,8192]{1,0:T(8,128)(2,1)} %q_hbm.1, bf16[128,512]{1,0:T(8,128)(2,1)} %k_hbm.1, bf16[128,512]{1,0:T(8,128)(2,1)} %v_hbm.1, s32[1,128]{1,0:T(1,128)} %bitcast.1), custom_call_target="tpu_custom_call" | custom-call | tf_op jit(solution)/shard_map/attention/pallas_call | solution.py:310
  36.9 1.3 %copy.8 = bf16[128,8192]{1,0:T(8,128)(2,1)} copy(bf16[128,8192]{1,0:T(8,128)(2,1)S(1)} %get-tuple-element.2) | data formatting | bytes 4194304
  38.3 0.6 %copy.9 = f32[64,128]{1,0:T(8,128)} copy(f32[64,128]{1,0:T(8,128)S(1)} %get-tuple-element.3) | data formatting | bytes 65536
